TPU v7x, 32 devices: a whole 2x2x4 slice. The times are simulated.
32 devices in a mesh: chol: 4 (over y, x), pair: 8 (over z, core).
Axes of the slice: x: 2, y: 2, z: 4, core: 2. Of those that a mesh axis runs over, the one named last changes fastest.
Arguments:
- green: bfloat16 [2, 128, 147456], P(None, 'chol', 'pair'), may hold values from -6 to 6
- chol_rot: bfloat16 [147456, 1024], P('pair', 'chol'), may hold values from -0.015625 to 0.015625
Outputs:
- force_bias: float32 [2, 128, 1024], P(None, 'pair', 'chol')
All inputs are finite; a program needn't handle non-finite values.
Results may differ from a plain program's by a relative error of at most 0.0003.
Values may be sent and summed in bfloat16 or wider, within the bound.
A program may use at most 64 MiB of HBM per device.

v0:
```python
import jax
import jax.numpy as jnp
from jax import lax
from jax.sharding import PartitionSpec as P


def local(green, chol_rot):
    partial_value = jnp.einsum(
        "cwp,pg->wcg",
        lax.all_gather(green, "chol", axis=1, tiled=True),
        chol_rot,
        preferred_element_type=jnp.float32,
    )
    summed = lax.psum_scatter(partial_value, "pair", scatter_dimension=0, tiled=True)
    return jnp.transpose(summed, (1, 0, 2))


def solution(mesh):
    return jax.shard_map(
        local,
        mesh=mesh,
        in_specs=(P(None, "chol", "pair"), P("pair", "chol")),
        out_specs=P(None, "pair", "chol"),
        check_vma=False,
    )
```

profile of v0, /device:TPU:0, one launch (start us, length us, event | category | flops | bytes accessed | tf_op | source)
XLA Modules:
  0.0 182.8 jit_solution(14260340009630837000)
XLA Ops:
  6.5 0.0 all-gather.2.cloned.1.call-start
  6.5 0.7 all-gather.2.cloned.1.call-update
  7.3 0.0 copy-start
  7.3 0.0 all-reduce.3.cloned.1.call-start
  7.3 101.0 %all-gather.2.cloned.1.call-done = bf16[2,128,18432]{2,1,0:T(8,128)(2,1)} async-done(((bf16[2,32,18432]{2,1,0:T(8,128)(2,1)}), bf16[2,128,18432]{2,1,0:T(8,128)(2,1)}) %all-gather.2.cloned.1.call-update) | async-done | bytes 9437200 | tf_op jit(solution)/shard_map/all_gather | solution.py:10
  108.3 10.4 %fusion.2 = f32[128,2,256]{0,2,1:T(8,128)S(1)} fusion(bf16[2,128,18432]{2,1,0:T(8,128)(2,1)} %all-gather.2.cloned.1.call-done, bf16[18432,256]{1,0:T(8,128)(2,1)} %param.3), kind=kOutput, calls=%fused_computation.2 | convolution fusion | flops 2415919104 | bytes 19136512 | tf_op jit(solution)/shard_map/cwp,pg->wcg/dot_general | solution.py:8
  118.7 0.8 copy.6
  119.5 0.0 all-reduce.3.cloned.1.call-update
  119.5 0.0 copy-done
  119.6 0.6 dynamic-slice
  120.8 53.8 %all-reduce.3.cloned.1.call-done = f32[128,2,256]{2,1,0:T(2,128)} async-done(((f32[128,2,256]{2,1,0:T(2,128)}), f32[128,2,256]{2,1,0:T(2,128)}) %all-reduce.3.cloned.1.call-update) | async-done | bytes 262160
  174.6 0.8 dynamic-slice_bitcast_fusion
  175.3 0.6 copy.7
Async XLA Ops:
  6.5 101.7 %all-gather.2.cloned.1.call-start = ((), (), s32[]{:S(2)}) async-start(), calls=%async_computation | async-start | bytes 11796480 | tf_op jit(solution)/shard_map/all_gather | solution.py:10
  7.3 112.3 %copy-start = (u32[32]{0:T(128)S(1)}, u32[32]{0:T(128)}, u32[]{:S(2)}) copy-start(u32[32]{0:T(128)} %constant.2) | copy-start | bytes 388
  7.3 167.3 %all-reduce.3.cloned.1.call-start = ((), (), s32[]{:S(2)}) async-start(), calls=%async_computation.1 | async-start | bytes 524288
Sparse Core Ops, SparseCore 0:
  9.2 99.0 all-gather.1
  119.7 54.8 all-reduce.2
where the time goes:
time: 183 us
  waiting for transfers between devices  155 us (85%)
  between operations  14.1 us (8%)
  matrix products  10.4 us (6%)
  local copies, waits for them, and re-layouts  2.81 us (2%)
    all_gather x1, waiting for transfers between devices, local(): lax.all_gather(green, 'chol', axis=1, tiled=True)  101 us
    unnamed x3, waiting for transfers between devices  54.5 us
    dot_general x1, matrix products, local(): jnp.einsum('cwp,pg->wcg', lax.all_gather(green, 'chol', axis=1, tiled=Tru...  10.4 us
  transfers between devices with their start and end apart: 2, of which 2 were waited for; matrix products, arithmetic and copies ran while one was open for 0% of the time, Pallas kernels for 0%

commit v1 on v0

--- a/solution.py
+++ b/solution.py
@@ -4,12 +4,22 @@
 from jax.sharding import PartitionSpec as P
 
 
+def gather_around(array, axis, dim):
+    ways = lax.axis_size(axis)
+    up = [(d, (d + 1) % ways) for d in range(ways)]
+    down = [(d, (d - 1) % ways) for d in range(ways)]
+    earlier, later = ([array], [array])
+    for _ in range(ways // 2):
+        earlier.append(lax.ppermute(earlier[-1], axis, up))
+    for _ in range((ways - 1) // 2):
+        later.append(lax.ppermute(later[-1], axis, down))
+    line = jnp.concatenate([*earlier[::-1], *later[1:]], axis=dim)
+    return jnp.roll(line, (lax.axis_index(axis) - ways // 2) * array.shape[dim], axis=dim)
+
+
 def local(green, chol_rot):
     partial_value = jnp.einsum(
-        "cwp,pg->wcg",
-        lax.all_gather(green, "chol", axis=1, tiled=True),
-        chol_rot,
-        preferred_element_type=jnp.float32,
+        "cwp,pg->wcg", gather_around(green, "chol", 1), chol_rot, preferred_element_type=jnp.float32
     )
     summed = lax.psum_scatter(partial_value, "pair", scatter_dimension=0, tiled=True)
     return jnp.transpose(summed, (1, 0, 2))

time: 183 us -> 218 us (1.19)
  waiting for transfers between devices: 155 us -> 178 us
  local copies, waits for them, and re-layouts: 2.81 us -> 12.9 us
  starting transfers between devices: 0.04 us -> 5.87 us
  matrix products: 10.4 us -> 6.97 us
    ppermute x0 -> x3, waiting for transfers between devices: none -> 148 us  [the longest x2 105 us: gather_around(): earlier.append(lax.ppermute(earlier[-1], axis, up))]
    all_gather x1 -> x0, waiting for transfers between devices: 101 us -> none  [local(): lax.all_gather(green, 'chol', axis=1, tiled=True)]
    unnamed x3 -> x1, waiting for transfers between devices: 54.5 us -> 0.02 us
    reduce_scatter x0 -> x1, waiting for transfers between devices: none -> 29.9 us  [local(): lax.psum_scatter(partial_value, 'pair', scatter_dimension=0, tiled=True)]
    unnamed x3 -> x9, local copies, waits for them, and re-layouts: 0.59 us -> 11.1 us
    ppermute x0 -> x3, starting transfers between devices: none -> 5.86 us  [the longest x2 3.66 us: gather_around(): earlier.append(lax.ppermute(earlier[-1], axis, up))]
    dot_general x1, matrix products: 10.4 us -> 6.97 us  [local(): jnp.einsum('cwp,pg->wcg', gather_around(green, 'chol', 1), chol_rot, pref...]
    transpose x3 -> x0, local copies, waits for them, and re-layouts: 2.21 us -> none  [the longest x2 1.38 us: local(): return jnp.transpose(summed, (1, 0, 2))]
  transfers between devices with their start and end apart: 2 -> 4, of which waited for: 2 -> 4; matrix products, arithmetic and copies ran while one was open for 0% -> 3% of each run, Pallas kernels for 0% -> 0%
where the time goes in v1:
time: 218 us; the launch traced here: 217 us
  waiting for transfers between devices  178 us (82%)
  between operations  13.4 us (6%)
  local copies, waits for them, and re-layouts  12.9 us (6%)
  matrix products  6.97 us (3%)
  starting transfers between devices  5.87 us (3%)
    ppermute x2, waiting for transfers between devices, gather_around(): earlier.append(lax.ppermute(earlier[-1], axis, up))  105 us
    ppermute x1, waiting for transfers between devices, gather_around(): later.append(lax.ppermute(later[-1], axis, down))  43.2 us
    reduce_scatter x1, waiting for transfers between devices, local(): lax.psum_scatter(partial_value, 'pair', scatter_dimension=0, tiled=True)  29.9 us
    unnamed x9, local copies, waits for them, and re-layouts  11.1 us
    dot_general x1, matrix products, local(): jnp.einsum('cwp,pg->wcg', gather_around(green, 'chol', 1), chol_rot, pref...  6.97 us
  transfers between devices with their start and end apart: 4, of which 4 were waited for; matrix products, arithmetic and copies ran while one was open for 3% of the time, Pallas kernels for 0%

profile of v1, /device:TPU:0, one launch (start us, length us, event | category | flops | bytes accessed | tf_op | source)
XLA Modules:
  0.0 217.4 jit_solution(15633685500396896558)
XLA Ops:
  6.5 0.0 copy-start
  6.5 0.0 reduce-scatter.2.cloned.1.call-start
  6.5 2.9 %collective-permute-start = (bf16[2,32,18432]{2,1,0:T(8,128)(2,1)}, bf16[2,32,18432]{2,1,0:T(8,128)(2,1)}, u32[]{:S(2)}, u32[]{:S(2)}) collective-permute-start(bf16[2,32,18432]{2,1,0:T(8,128)(2,1)} %param.2), channel_id=1, source_target_pairs={{0,8},{8,16},{16,24},{24,0},{1,9},{9,17},{17,25},{25,1},{2,10},{10... | collective-permute-start | bytes 7077896 | tf_op jit(solution)/shard_map/ppermute | solution.py:13
  9.5 52.6 %collective-permute-done = bf16[2,32,18432]{2,1,0:T(8,128)(2,1)} collective-permute-done((bf16[2,32,18432]{2,1,0:T(8,128)(2,1)}, bf16[2,32,18432]{2,1,0:T(8,128)(2,1)}, u32[]{:S(2)}, u32[]{:S(2)}) %collective-permute-start) | collective-permute-done | bytes 2359328 | tf_op jit(solution)/shard_map/ppermute | solution.py:13
  62.1 0.7 collective-permute-start.1
  62.8 2.2 %collective-permute-start.2 = (bf16[2,32,18432]{2,1,0:T(8,128)(2,1)}, bf16[2,32,18432]{2,1,0:T(8,128)(2,1)}, u32[]{:S(2)}, u32[]{:S(2)}) collective-permute-start(bf16[2,32,18432]{2,1,0:T(8,128)(2,1)} %param.2), channel_id=1, source_target_pairs={{0,24},{8,0},{16,8},{24,16},{1,25},{9,1},{17,9},{25,17},{2,26},{10... | collective-permute-start | bytes 7077896 | tf_op jit(solution)/shard_map/ppermute | solution.py:15
  65.0 52.5 %collective-permute-done.1 = bf16[2,32,18432]{2,1,0:T(8,128)(2,1)} collective-permute-done((bf16[2,32,18432]{2,1,0:T(8,128)(2,1)}, bf16[2,32,18432]{2,1,0:T(8,128)(2,1)}, u32[]{:S(2)}, u32[]{:S(2)}) %collective-permute-start.1) | collective-permute-done | bytes 2359328 | tf_op jit(solution)/shard_map/ppermute | solution.py:13
  117.5 1.8 constant_dynamic-update-slice_fusion.7
  119.3 1.8 constant_dynamic-update-slice_fusion.6
  121.1 1.8 constant_dynamic-update-slice_fusion.5
  122.9 43.2 %collective-permute-done.2 = bf16[2,32,18432]{2,1,0:T(8,128)(2,1)} collective-permute-done((bf16[2,32,18432]{2,1,0:T(8,128)(2,1)}, bf16[2,32,18432]{2,1,0:T(8,128)(2,1)}, u32[]{:S(2)}, u32[]{:S(2)}) %collective-permute-start.2) | collective-permute-done | bytes 2359328 | tf_op jit(solution)/shard_map/ppermute | solution.py:15
  166.1 1.8 constant_dynamic-update-slice_fusion.4
  168.0 1.8 constant_dynamic-update-slice_fusion.3
  169.8 1.8 constant_dynamic-update-slice_fusion.2
  171.6 0.0 copy-done
  171.6 0.2 constant_dynamic-update-slice_fusion.1
  171.8 1.8 constant_dynamic-update-slice_fusion
  173.6 7.0 %fusion.3 = f32[128,2,256]{2,0,1:T(8,128)} fusion(bf16[18432,256]{1,0:T(8,128)(2,1)} %param.3, bf16[2,256,18432]{2,1,0:T(8,128)(2,1)S(1)} %constant_dynamic-update-slice_fusion, s32[]{:T(128)S(6)} %select_n.14), kind=kOutput, calls=%fused_computation.3 | convolution fusion | flops 2415919104 | bytes 19136516 | tf_op jit(solution)/shard_map/cwp,pg->wcg/dot_general | solution.py:21
  180.6 0.0 reduce-scatter.2.cloned.1.call-update
  180.6 29.9 %reduce-scatter.2.cloned.1.call-done = f32[16,2,256]{2,0,1:T(8,128)} async-done(((f32[128,2,256]{2,0,1:T(8,128)}), f32[16,2,256]{2,0,1:T(8,128)}) %reduce-scatter.2.cloned.1.call-update) | async-done | bytes 32784 | tf_op jit(solution)/shard_map/reduce_scatter | solution.py:24
Async XLA Ops:
  6.5 165.1 %copy-start = (bf16[2,32,18432]{2,1,0:T(8,128)(2,1)S(1)}, bf16[2,32,18432]{2,1,0:T(8,128)(2,1)}, u32[]{:S(2)}) copy-start(bf16[2,32,18432]{2,1,0:T(8,128)(2,1)} %param.2) | copy-start | bytes 7077892
  6.5 204.0 %reduce-scatter.2.cloned.1.call-start = ((), (), s32[]{:S(2)}) async-start(), calls=%async_computation.1 | async-start | bytes 294912 | tf_op jit(solution)/shard_map/reduce_scatter | solution.py:24
  6.5 55.5 %collective-permute-start = (bf16[2,32,18432]{2,1,0:T(8,128)(2,1)}, bf16[2,32,18432]{2,1,0:T(8,128)(2,1)}, u32[]{:S(2)}, u32[]{:S(2)}) collective-permute-start(bf16[2,32,18432]{2,1,0:T(8,128)(2,1)} %param.2), channel_id=1, source_target_pairs={{0,8},{8,16},{16,24},{24,0},{1,9},{9,17},{17,25},{25,1},{2,10},{10... | collective-permute-start | bytes 7077896 | tf_op jit(solution)/shard_map/ppermute | solution.py:13
  62.1 55.4 %collective-permute-start.1 = (bf16[2,32,18432]{2,1,0:T(8,128)(2,1)}, bf16[2,32,18432]{2,1,0:T(8,128)(2,1)}, u32[]{:S(2)}, u32[]{:S(2)}) collective-permute-start(bf16[2,32,18432]{2,1,0:T(8,128)(2,1)} %collective-permute-done), channel_id=1, source_target_pairs={{0,8},{8,16},{16,24},{24,0},{1,9},{9,17},{17,25},{25,1},{2,10},{10... | collective-permute-start | bytes 7077896 | tf_op jit(solution)/shard_map/ppermute | solution.py:13
  62.8 103.4 %collective-permute-start.2 = (bf16[2,32,18432]{2,1,0:T(8,128)(2,1)}, bf16[2,32,18432]{2,1,0:T(8,128)(2,1)}, u32[]{:S(2)}, u32[]{:S(2)}) collective-permute-start(bf16[2,32,18432]{2,1,0:T(8,128)(2,1)} %param.2), channel_id=1, source_target_pairs={{0,24},{8,0},{16,8},{24,16},{1,25},{9,1},{17,9},{25,17},{2,26},{10... | collective-permute-start | bytes 7077896 | tf_op jit(solution)/shard_map/ppermute | solution.py:15
Sparse Core Ops, SparseCore 0:
  180.7 29.7 reduce-scatter.1
